TPU v7x, 256 devices: a whole 4x4x8 slice. The times are simulated.
256 devices in a mesh: ia: 16 (over z, y_lo), ja: 16 (over y_hi, x, core).
Axes of the slice: x: 4, y: 4 (y_hi: 2, y_lo: 2; y = y_hi * 2 + y_lo), z: 8, core: 2. Of those that a mesh axis runs over, the one named last changes fastest.
Arguments:
- amplitudes: float32 [64, 64, 384, 384], P('ia', 'ja'), may hold values from -6 to 6
- integrals: float32 [768, 384, 384], P('ia', 'ja'), may hold values from -0.0625 to 0.0625
- occ_irrep: int32 [64], replicated, may hold values from 0 to 7
- vir_irrep: int32 [6], replicated, may hold values from 0 to 7
- occ_energy: float32 [64], replicated, may hold values from -2 to -0.3
- vir_energy: float32 [384], replicated, may hold values from 0.2 to 2.5
Outputs:
- residual: float32 [64, 64, 768], P('ia', None, 'ja')
All inputs are finite; a program needn't handle non-finite values.
Results may differ from a plain program's by a relative error of at most 0.0003.
Values sent between devices are 32-bit elements; how exact they have to be, the bound alone decides.
No kernel may reach another device: no remote copies, remote signals or barrier semaphores. Data moves between devices by JAX's collectives and lax.ppermute only.
A program may use at most 192 MiB of HBM per device.

v0:
```python
import functools

import jax
import jax.numpy as jnp
from jax import lax
from jax.experimental import pallas as pl
from jax.experimental.pallas import tpu as pltpu
from jax.sharding import Mesh, PartitionSpec as P

O = 64
NV = 384
VT = 64
SA = 2
NVT = NV // VT
Z = 8
YL = 2
JA = 16
NI = 4
PAIRS = NI * NI
CB = NV // JA
CK = CB // YL
AB = SA * NV // (Z * YL)
ROWS = JA * PAIRS
GROUP = 4
LANES = 128
MIB = 1024 * 1024
KEPT = 64


def layout(slots):
    return [(2 * t, 2 * t + 1) for t in range(slots // 2)] + [(slots - 1, slots - 1)] * (slots % 2)


def lane_tiles(slots):
    return CK * slots // 2


def slot_tiles(wanted, vir, slots):
    lane = lax.broadcasted_iota(jnp.int32, wanted.shape, wanted.ndim - 1)
    slot = jnp.where(lane < VT, slots[0], slots[1])
    count = jnp.zeros(wanted.shape, jnp.int32)
    chosen = jnp.full(wanted.shape, -1, jnp.int32)
    for td in range(NVT):
        match = wanted == vir[td]
        chosen = jnp.where(match & (count == slot), td, chosen)
        count = jnp.where(match, count + 1, count)
    return chosen


def straight_and_turned(chosen):
    half = (lax.broadcasted_iota(jnp.int32, chosen.shape, chosen.ndim - 1) >= VT).astype(jnp.int32)
    return [
        jnp.where((each >= 0) & ((each & 1) == half), each >> 1, -1)
        for each in (chosen, pltpu.roll(chosen, VT, chosen.ndim - 1))
    ]


def pack_tiles(block, chosen_of):
    packed = {}
    for key, chosen in chosen_of.items():
        terms = []
        for each in chosen:
            term = jnp.zeros(block.shape[:2] + (LANES,), jnp.float32)
            for k in range(NV // LANES):
                term = jnp.where(each == k, block[:, :, k * LANES : (k + 1) * LANES], term)
            terms.append(term)
        packed[key] = terms[0] + pltpu.roll(terms[1], VT, 2)
    return packed


def store_tiles(slots, rows, b, packed, out_ref):
    full = slots // 2
    depth = lane_tiles(slots)

    def store(c, tile, values):
        out_ref[pl.ds(((c // CK) * depth + tile) * rows, rows), :] = values

    for t, key in enumerate(layout(slots)):
        values = packed[key]
        if t == full:
            low = lax.broadcasted_iota(jnp.int32, values.shape, 2) < VT
            values = jnp.where(low, values, pltpu.roll(values, 6, 1))
        values = jnp.swapaxes(values, 0, 1)
        for r in range(8):
            c = 8 * b + r
            if t < full:
                store(c, (c % CK) * full + t, values[r])
            elif r % 4 < 2:
                store(c, CK * full + (c % CK) // 4 * 2 + r % 4, values[r])


def pack_amplitudes_kernel(slots, occ, vir, t_ref, out_ref, chosen_ref):
    step = pl.program_id(0)
    keys = layout(slots)

    @pl.when(step == 0)
    def _():
        first_i = NI * (YL * lax.axis_index("z") + lax.axis_index("yl"))
        first_j = NI * lax.axis_index("ja")

        pair = lax.broadcasted_iota(jnp.int32, (PAIRS, 8, LANES), 0)
        labels = jnp.zeros(pair.shape, jnp.int32)
        for p in range(PAIRS):
            labels = jnp.where(pair == p, occ[first_i + p // NI] ^ occ[first_j + p % NI], labels)

        @pl.loop(0, NVT)
        def _(tc):
            for n, key in enumerate(keys):
                chosen_ref[tc, n, 0], chosen_ref[tc, n, 1] = straight_and_turned(slot_tiles(labels ^ vir[tc], vir, key))

    @pl.loop(0, GROUP)
    def _(g):
        for b in range(CB // 8):
            tc = ((step * GROUP + g) * (CB // 8) + b) // (VT // 8)
            chosen_of = {key: (chosen_ref[tc, n, 0], chosen_ref[tc, n, 1]) for n, key in enumerate(keys)}
            packed = pack_tiles(t_ref[:, pl.ds(pl.multiple_of(g * CB + b * 8, 8), 8), :], chosen_of)
            store_tiles(slots, PAIRS, b, packed, out_ref.at[g])


def pack_amplitudes(amplitudes, occ_irrep, vir_irrep, slots):
    rows = YL * lane_tiles(slots) * PAIRS
    return pl.pallas_call(
        functools.partial(pack_amplitudes_kernel, slots),
        out_shape=jax.ShapeDtypeStruct((JA, rows, LANES), jnp.float32),
        grid=(JA // GROUP,),
        in_specs=[
            pl.BlockSpec(memory_space=pltpu.SMEM),
            pl.BlockSpec(memory_space=pltpu.SMEM),
            pl.BlockSpec((PAIRS, GROUP * CB, NV), lambda s: (0, s, 0)),
        ],
        out_specs=pl.BlockSpec((GROUP, rows, LANES), lambda s: (s, 0, 0)),
        scratch_shapes=[pltpu.VMEM((NVT, len(layout(slots)), 2, PAIRS, 8, LANES), jnp.int32)],
        compiler_params=pltpu.CompilerParams(vmem_limit_bytes=20 * MIB),
        cost_estimate=pl.CostEstimate(flops=10**7, bytes_accessed=14 * 10**6, transcendentals=0),
    )(occ_irrep, vir_irrep, amplitudes.reshape(PAIRS, NV, NV))


def pack_integrals_kernel(slots, vir, v_ref, kept_ref, sent_ref, packed_ref):
    ia = YL * lax.axis_index("z") + lax.axis_index("yl")
    tb = (AB * (ia % (Z * YL // SA)) + 16 * pl.program_id(0)) // VT
    for b in range(CB // 8):
        tc = (lax.axis_index("ja") * (CB // 8) + b) // (VT // 8)
        wanted = jnp.full((8, LANES), vir[0] ^ vir[tb] ^ vir[tc], jnp.int32)
        chosen_of = {key: straight_and_turned(slot_tiles(wanted, vir, key)) for key in layout(slots)}
        store_tiles(slots, 16, b, pack_tiles(v_ref[:, b * 8 : (b + 1) * 8, :], chosen_of), packed_ref)
    depth = lane_tiles(slots) * 16
    for yl, ref in ((lax.axis_index("yl"), kept_ref), (1 - lax.axis_index("yl"), sent_ref)):
        ref[...] = packed_ref[pl.ds(pl.multiple_of(yl * depth, 16), depth), :].reshape(ref.shape)


def pack_integrals(integrals, vir_irrep, slots):
    depth = lane_tiles(slots)
    return pl.pallas_call(
        functools.partial(pack_integrals_kernel, slots),
        out_shape=[jax.ShapeDtypeStruct((depth, AB, LANES), jnp.float32)] * 2,
        grid=(AB // 16,),
        in_specs=[
            pl.BlockSpec(memory_space=pltpu.SMEM),
            pl.BlockSpec((16, CB, NV), lambda s: (s, 0, 0)),
        ],
        out_specs=[pl.BlockSpec((depth, 16, LANES), lambda s: (0, s, 0))] * 2,
        scratch_shapes=[pltpu.VMEM((YL * depth * 16, LANES), jnp.float32)],
        compiler_params=pltpu.CompilerParams(vmem_limit_bytes=12 * MIB),
        cost_estimate=pl.CostEstimate(flops=10**6, bytes_accessed=3 * 10**6, transcendentals=0),
    )(vir_irrep, integrals)


def split(values):
    high = values.astype(jnp.bfloat16)
    return high, (values - high.astype(jnp.float32)).astype(jnp.bfloat16)


def dot(left, right, right_dim):
    return lax.dot_general(left, right, (((1,), (right_dim,)), ((), ())), preferred_element_type=jnp.float32)


def place(values, chosen, right_dim):
    terms = dot(jnp.concatenate(split(values), axis=0), chosen, right_dim)
    return terms[: values.shape[0]] + terms[values.shape[0] :]


def kept_rows(labels, wanted):
    at = lax.broadcasted_iota(jnp.int32, (8, ROWS), 0)
    label_of = jnp.zeros((8, ROWS), jnp.int32)
    for n, label in enumerate(wanted):
        label_of = jnp.where(at == n, label, label_of)
    match = (label_of == labels) & (at < len(wanted))
    before = lax.broadcasted_iota(jnp.int32, (ROWS, ROWS), 0) < lax.broadcasted_iota(jnp.int32, (ROWS, ROWS), 1)
    rank = dot(jnp.where(match, 1.0, 0.0).astype(jnp.bfloat16), jnp.where(before, 1.0, 0.0).astype(jnp.bfloat16), 0)
    rank = jnp.where(match, rank.astype(jnp.int32), -ROWS)
    slot = lax.broadcasted_iota(jnp.int32, (LANES, ROWS), 0)
    return [
        [jnp.where(rank[n : n + 1] + shift == slot, 1.0, 0.0).astype(jnp.bfloat16) for shift in (0, KEPT)]
        for n in range(len(wanted))
    ]


HOPS = [(other, side * n) for n in range(1, 4) for other in range(YL) for side in (1, -1)] + [(0, 4), (1, -4)]
RING = sorted([(0, 0), (1, 0)] + HOPS, key=lambda of: (of[1] % Z, of[0]))
BLOCKS = SA * NV // 16
TILE_BLOCKS = VT // 16


def contract_kernel(keep_all, vir, labels_ref, t_ref, *refs):
    v_refs, (out_ref, v_held, sem, v_high, v_low, t_high, t_low, sums_ref, kept_ref) = refs[:-9], refs[-9:]
    depth = t_ref.shape[2]

    copies, first = [], 0
    for v_ref in v_refs:
        copies.append(pltpu.make_async_copy(v_ref, v_held.at[pl.ds(first, v_ref.shape[0])], sem.at[first]))
        first += v_ref.shape[0]

    @pl.when(pl.program_id(0) == 0)
    def _():
        for copy in copies:
            copy.start()

    labels = labels_ref[0]
    wanted = [vir[0] ^ vir[tb] for tb in range(NVT)]
    if not keep_all:
        for tb, matrices in enumerate(kept_rows(labels, wanted)):
            for n, matrix in enumerate(matrices):
                kept_ref[tb, :, n * ROWS : (n + 1) * ROWS] = matrix

    @pl.loop(0, depth)
    def _(k):
        at = pl.ds(pl.multiple_of(k * LANES, LANES), LANES)
        t_high[:, at], t_low[:, at] = split(t_ref[:, 0, k].reshape(ROWS, LANES))

    @pl.when(pl.program_id(0) == 0)
    def _():
        for copy in copies:
            copy.wait()

        @pl.loop(0, depth)
        def _(k):
            at = pl.ds(pl.multiple_of(k * LANES, LANES), LANES)
            v_high[:, at], v_low[:, at] = split(v_held[:, k].reshape(SA * NV, LANES))

    part = 384

    @pl.loop(0, SA * NV // part)
    def _(m):
        at = pl.ds(pl.multiple_of(m * part, part), part)
        high, low = v_high[at], v_low[at]
        total = dot(high, t_high[...], 1) + dot(high, t_low[...], 1) + dot(low, t_high[...], 1)
        sums_ref[pl.ds(m * (part // 16), part // 16)] = total.reshape(part // 16, 16, ROWS)

    z, yl = lax.axis_index("z"), lax.axis_index("yl")

    def sums_at(block):
        source = block // 3
        return 3 * (YL * lax.rem(z - source // YL + Z, Z) + (yl ^ (source % YL))) + block % 3

    if keep_all:
        for n in range(BLOCKS):
            kept = jnp.where(labels == wanted[n % (BLOCKS // SA) // TILE_BLOCKS], sums_ref[sums_at(n)], 0.0)
            out_ref[0, n // 3, 16 * (n % 3) : 16 * (n % 3) + 16, :] = kept
        return
    for tb in range(NVT):
        blocks = [a * (BLOCKS // SA) + tb * TILE_BLOCKS + q for a in range(SA) for q in range(TILE_BLOCKS)]
        sums = [sums_ref[sums_at(n)] for n in blocks]
        sums = jnp.concatenate([jnp.concatenate([each[:8], each[8:]], axis=1) for each in sums], axis=0)
        kept = place(sums, kept_ref[tb], 1)
        for m, n in enumerate(blocks):
            out_ref[0, n // 3, 8 * (n % 3) : 8 * (n % 3) + 8, :] = kept[8 * m : 8 * m + 8]


def contract(received, ring, labels, vir_irrep, slots, keep_all):
    depth = lane_tiles(slots)
    rest = (AB, ROWS) if keep_all else (AB // 2, LANES)
    return pl.pallas_call(
        functools.partial(contract_kernel, keep_all),
        out_shape=jax.ShapeDtypeStruct((YL, JA) + rest, jnp.float32),
        grid=(YL,),
        in_specs=[
            pl.BlockSpec(memory_space=pltpu.SMEM),
            pl.BlockSpec((1, 1, ROWS), lambda s: (s, 0, 0)),
            pl.BlockSpec((JA, 1, depth, PAIRS, LANES), lambda s: (0, s, 0, 0, 0)),
        ]
        + [pl.BlockSpec(memory_space=pl.ANY)] * len(ring),
        out_specs=pl.BlockSpec((1, JA) + rest, lambda s: (s, 0, 0, 0)),
        scratch_shapes=[pltpu.VMEM((Z * YL, depth, AB, LANES), jnp.float32), pltpu.SemaphoreType.DMA((Z * YL,))]
        + [pltpu.VMEM((Z * YL * AB, depth * LANES), jnp.bfloat16)] * 2
        + [pltpu.VMEM((ROWS, depth * LANES), jnp.bfloat16)] * 2
        + [pltpu.VMEM((BLOCKS, 16, ROWS), jnp.float32), pltpu.VMEM((NVT, LANES, 2 * ROWS), jnp.bfloat16)],
        compiler_params=pltpu.CompilerParams(vmem_limit_bytes=60 * MIB),
        cost_estimate=pl.CostEstimate(flops=6 * 768 * 512 * LANES * depth, bytes_accessed=10**7, transcendentals=0),
    )(vir_irrep, labels, received, *ring)


def reduce_kernel(keep_all, vir, labels_ref, parts_ref, out_ref):
    total = parts_ref[0]
    for n in range(1, YL * JA):
        total += parts_ref[n]
    if keep_all:
        rows = [total]
    else:
        first_block = lax.axis_index("ja") * (AB // 16)
        wanted = [vir[0] ^ vir[(first_block + g) % (BLOCKS // SA) // TILE_BLOCKS] for g in range(AB // 16)]
        rows = []
        for g, chosen in enumerate(kept_rows(labels_ref[lax.axis_index("yl")], wanted)):
            rows += [place(total[8 * g : 8 * g + 8], each, 0) for each in chosen]
    out_ref[...] = jnp.concatenate(rows + [jnp.zeros((LANES - AB, ROWS), jnp.float32)], axis=0).T


def reduce_parts(parts, labels, vir_irrep, keep_all):
    whole = pl.BlockSpec(memory_space=pltpu.VMEM)
    return pl.pallas_call(
        functools.partial(reduce_kernel, keep_all),
        out_shape=jax.ShapeDtypeStruct((ROWS, LANES), jnp.float32),
        in_specs=[pl.BlockSpec(memory_space=pltpu.SMEM), whole, whole],
        out_specs=whole,
        compiler_params=pltpu.CompilerParams(vmem_limit_bytes=12 * MIB),
    )(vir_irrep, labels, parts)


def finish(ladder, occ_energy, vir_energy):
    z, yl, ja = lax.axis_index("z"), lax.axis_index("yl"), lax.axis_index("ja")
    mirror = lax.all_to_all(ladder, ("z", "yl"), split_axis=0, concat_axis=0, tiled=True)
    ladder = ladder.reshape(JA, NI, NI, LANES)[..., :AB].transpose(1, 0, 2, 3).reshape(NI, O, AB)
    mirror = mirror.reshape(JA, NI, NI, LANES)[..., :AB].transpose(2, 0, 1, 3).reshape(NI, O, AB)
    ab_energy = (vir_energy[:SA, None] + vir_energy[None, :]).reshape(SA * NV)
    ab_part = lax.dynamic_slice_in_dim(ab_energy, ja * AB, AB)
    occ_part = lax.dynamic_slice_in_dim(occ_energy, NI * (YL * z + yl), NI)
    denominator = occ_part[:, None, None] + occ_energy[None, :, None] - ab_part[None, None, :]
    return (ladder - mirror) / denominator


def ladder_rows(slots, whole, keep_all, amplitudes, integrals, occ_irrep, vir_irrep):
    forward = [(n, (n + 1) % Z) for n in range(Z)]
    backward = [(n, (n - 1) % Z) for n in range(Z)]
    kept, sent = pack_integrals(integrals, vir_irrep, slots)
    neighbours = lax.ppermute(sent, "yl", [(0, 1), (1, 0)])
    if keep_all:
        both, occ_irrep = lax.optimization_barrier((jnp.stack([kept, neighbours]), occ_irrep))
        packed = pack_amplitudes(amplitudes, occ_irrep, vir_irrep, slots)

        def turn(n, carried):
            behind, ahead, blocks = carried
            behind, ahead = lax.ppermute(behind, "z", forward), lax.ppermute(ahead, "z", backward)
            blocks = lax.dynamic_update_index_in_dim(blocks, behind, n, 0)
            return behind, ahead, lax.dynamic_update_index_in_dim(blocks, ahead, Z - n, 0)

        blocks = jnp.broadcast_to(both, (Z,) + both.shape)
        blocks = lax.fori_loop(1, Z // 2 + 1, turn, (both, both, blocks))[2]
        ring = [blocks.reshape((Z * YL,) + kept.shape)]
    elif whole:
        packed = pack_amplitudes(amplitudes, occ_irrep, vir_irrep, slots)
        packed, neighbours = lax.optimization_barrier((packed, neighbours))
        blocks = {0: jnp.stack([kept, neighbours])}
        for n in range(1, Z // 2):
            blocks[n] = lax.ppermute(blocks[n - 1], "z", forward)
            blocks[-n] = lax.ppermute(blocks[1 - n], "z", backward)
        last = [lax.ppermute(blocks[3][:1], "z", forward), lax.ppermute(blocks[-3][1:], "z", backward)]
        ring = [*(blocks[n] for n in range(Z // 2)), *last, *(blocks[n - Z // 2] for n in range(1, Z // 2))]
    else:
        ring = {(0, 0): kept, (1, 0): neighbours}

        def hop(other, behind):
            side = 1 if behind > 0 else -1
            ring[other, behind] = lax.ppermute(ring[other, behind - side], "z", forward if side > 0 else backward)

        for of in HOPS[:2]:
            hop(*of)
        packed = pack_amplitudes(amplitudes, occ_irrep, vir_irrep, slots)
        packed, ring[1, 0], ring[0, 1], ring[0, -1] = lax.optimization_barrier((packed, ring[1, 0], ring[0, 1], ring[0, -1]))
        for of in HOPS[2:]:
            hop(*of)
        ring = [ring[key][None] for key in RING]
    received = lax.all_to_all(
        packed.reshape(JA * YL, lane_tiles(slots) * PAIRS, LANES), ("ja", "yl"), split_axis=0, concat_axis=0, tiled=True
    ).reshape(JA, YL, lane_tiles(slots), PAIRS, LANES)
    occ_rows = lax.dynamic_slice_in_dim(occ_irrep, YL * NI * lax.axis_index("z"), YL * NI).reshape(YL, 1, NI, 1)
    labels = jnp.bitwise_xor(occ_rows, occ_irrep.reshape(1, JA, 1, NI)).reshape(YL, 1, ROWS)
    parts = contract(received, ring, labels, vir_irrep, slots, keep_all)
    parts = lax.all_to_all(
        parts.reshape((YL * JA,) + parts.shape[2:]), ("yl", "ja"), split_axis=0, concat_axis=0, tiled=True
    )
    return reduce_parts(parts, labels, vir_irrep, keep_all)


def tier_kernel(occ, vir, out_ref):
    def largest_class(ref):
        def count(n, counts):
            one = lax.shift_left(1, 8 * (ref[n] & 3))
            return counts[0] + jnp.where(ref[n] < 4, one, 0), counts[1] + jnp.where(ref[n] < 4, 0, one)

        counts = lax.fori_loop(0, ref.shape[0], count, (jnp.int32(0), jnp.int32(0)), unroll=True)
        largest = jnp.int32(0)
        for four in counts:
            for n in range(4):
                largest = jnp.maximum(largest, lax.shift_right_logical(four, 8 * n) & 255)
        return largest

    out_ref[0] = jnp.where(largest_class(occ) <= KEPT // NI, jnp.minimum(jnp.maximum(largest_class(vir) - 2, 0), 2), 2)


def local(amplitudes, integrals, occ_irrep, vir_irrep, occ_energy, vir_energy):
    scalars = pl.BlockSpec(memory_space=pltpu.SMEM)
    tier = pl.pallas_call(
        tier_kernel, out_shape=jax.ShapeDtypeStruct((1,), jnp.int32), in_specs=[scalars] * 2, out_specs=scalars
    )(occ_irrep, vir_irrep)
    branches = [functools.partial(ladder_rows, *of) for of in ((2, False, False), (3, True, False), (NVT, True, True))]
    ladder = lax.switch(tier[0], branches, amplitudes, integrals, occ_irrep, vir_irrep)
    return finish(ladder.reshape(JA, PAIRS, LANES), occ_energy, vir_energy)


def solution(mesh):
    parts = Mesh(mesh.devices.reshape(Z, YL, JA), ("z", "yl", "ja"))
    rows = ("z", "yl")
    in_specs = (P(rows, "ja", None, None), P(rows, "ja", None), P(), P(), P(), P())
    return jax.shard_map(local, mesh=parts, in_specs=in_specs, out_specs=P(rows, None, "ja"), check_vma=False)
```

profile of v0, /device:TPU:1, one launch (start us, length us, event | category | flops | bytes accessed | tf_op | source)
XLA Modules:
  0.0 122.3 jit_solution(9200082256987025273)
XLA Ops:
  0.0 1.4 %shard_map.64 = s32[1]{0:T(128)} custom-call(s32[64]{0:T(128)} %occ.1, s32[6]{0:T(128)} %vir.1), custom_call_target="tpu_custom_call" | custom-call | tf_op jit(solution)/shard_map/pallas_call | solution.py:401
  2.1 104.5 %conditional.1 = (f32[256,128]{1,0:T(8,128)}) conditional(s32[]{:T(128)} %bitcast.35, (s32[64]{0:T(128)}, f32[4,4,384,384]{3,2,1,0:T(8,128)}, s32[6]{0:T(128)}, f32[48,24,384]{2,1,0:T(8,128)}) %tuple.31, (s32[64]{0:T(128)}, f32[4,4,384,384]{3,2,1,0:T(8,128)}, s32[6]{0:T(128)}, f32[48,24,384]{2,1,0:T(8,128)}) %tuple.31, (s32[6]{0:T(128)}, ...), branch_computations={%region_0.0_spmd, %region_1.0_spmd, %region_2.5_spmd} | conditional | flops 10883079168 | bytes 151084832 | solution.py:405
  2.1 2.7 %branch_0_fun.5 = (f32[12,48,128]{2,1,0:T(8,128)S(1)}, f32[12,48,128]{2,1,0:T(8,128)S(1)}) custom-call(s32[6]{0:T(128)} %get-tuple-element.106.vir, f32[48,24,384]{2,1,0:T(8,128)} %get-tuple-element.109.v_ref), custom_call_target="tpu_custom_call" | custom-call | flops 1000000 | bytes 3000000 | tf_op jit(solution)/shard_map/cond/branch_0_fun/pallas_call | solution.py:153
  4.8 2.5 %collective-permute-start.1 = (f32[12,48,128]{2,1,0:T(8,128)S(1)}, f32[12,48,128]{2,1,0:T(8,128)S(1)}, u32[]{:S(2)}, u32[]{:S(2)}) collective-permute-start(f32[12,48,128]{2,1,0:T(8,128)S(1)} %get-tuple-element.111), channel_id=1, source_target_pairs={{0,32},{32,64},{64,96},{96,128},{128,160},{160,192},{192,224},{224... | collective-permute-start | bytes 884744 | tf_op jit(solution)/shard_map/cond/branch_0_fun/ppermute | solution.py:362
  7.4 4.0 %collective-permute-start.2 = (f32[12,48,128]{2,1,0:T(8,128)S(1)}, f32[12,48,128]{2,1,0:T(8,128)S(1)}, u32[]{:S(2)}, u32[]{:S(2)}) collective-permute-start(f32[12,48,128]{2,1,0:T(8,128)S(1)} %get-tuple-element.111), channel_id=1, source_target_pairs={{0,224},{32,0},{64,32},{96,64},{128,96},{160,128},{192,160},{224,1... | collective-permute-start | bytes 884744 | tf_op jit(solution)/shard_map/cond/branch_0_fun/ppermute | solution.py:362
  11.4 1.3 %collective-permute-start = (f32[12,48,128]{2,1,0:T(8,128)S(1)}, f32[12,48,128]{2,1,0:T(8,128)S(1)}, u32[]{:S(2)}, u32[]{:S(2)}) collective-permute-start(f32[12,48,128]{2,1,0:T(8,128)S(1)} %get-tuple-element.110), channel_id=1, source_target_pairs={{0,16},{16,0},{1,17},{17,1},{2,18},{18,2},{3,19},{19,3},{4,20},{20... | collective-permute-start | bytes 884744 | tf_op jit(solution)/shard_map/cond/branch_0_fun/ppermute | solution.py:334
  12.7 7.8 %branch_0_fun.4 = f32[16,384,128]{2,1,0:T(8,128)} custom-call(s32[64]{0:T(128)S(1)} %copy-done.13, s32[6]{0:T(128)S(1)} %copy-done.10, f32[16,384,384]{2,1,0:T(8,128)} %bitcast.60), custom_call_target="tpu_custom_call" | custom-call | flops 10000000 | bytes 14000000 | tf_op jit(solution)/shard_map/cond/branch_0_fun/pallas_call | solution.py:122
  20.5 0.7 copy-done.23
  21.3 0.7 copy-done.24
  22.0 8.0 %all-to-all-start = ((f32[32,192,128]{2,1,0:T(8,128)}), f32[32,192,128]{2,1,0:T(8,128)S(1)}, u32[]{:S(2)}, u32[]{:S(2)}) async-start(f32[32,192,128]{2,1,0:T(8,128)} %bitcast.1), calls=%async_computation | async-start | bytes 6291456 | tf_op jit(solution)/shard_map/cond/branch_0_fun/all_to_all | solution.py:371
  30.0 1.7 %collective-permute-start.9 = (f32[12,48,128]{2,1,0:T(8,128)}, f32[12,48,128]{2,1,0:T(8,128)S(1)}, u32[]{:S(2)}, u32[]{:S(2)}) collective-permute-start(f32[12,48,128]{2,1,0:T(8,128)} %copy-done.24), channel_id=1, source_target_pairs={{0,224},{32,0},{64,32},{96,64},{128,96},{160,128},{192,160},{224,1... | collective-permute-start | bytes 884744 | tf_op jit(solution)/shard_map/cond/branch_0_fun/ppermute | solution.py:362
  31.8 6.9 %collective-permute-done.9 = f32[12,48,128]{2,1,0:T(8,128)S(1)} collective-permute-done((f32[12,48,128]{2,1,0:T(8,128)}, f32[12,48,128]{2,1,0:T(8,128)S(1)}, u32[]{:S(2)}, u32[]{:S(2)}) %collective-permute-start.9) | collective-permute-done | bytes 294944 | tf_op jit(solution)/shard_map/cond/branch_0_fun/ppermute | solution.py:362
  38.7 2.9 %collective-permute-start.10 = (f32[12,48,128]{2,1,0:T(8,128)S(1)}, f32[12,48,128]{2,1,0:T(8,128)S(1)}, u32[]{:S(2)}, u32[]{:S(2)}) collective-permute-start(f32[12,48,128]{2,1,0:T(8,128)S(1)} %collective-permute-done.9), channel_id=1, source_target_pairs={{0,224},{32,0},{64,32},{96,64},{128,96},{160,128},{192,160},{224,1... | collective-permute-start | bytes 884744 | tf_op jit(solution)/shard_map/cond/branch_0_fun/ppermute | solution.py:362
  41.6 1.4 %collective-permute-start.5 = (f32[12,48,128]{2,1,0:T(8,128)S(1)}, f32[12,48,128]{2,1,0:T(8,128)}, u32[]{:S(2)}, u32[]{:S(2)}) collective-permute-start(f32[12,48,128]{2,1,0:T(8,128)S(1)} %collective-permute-done.3), channel_id=1, source_target_pairs={{0,32},{32,64},{64,96},{96,128},{128,160},{160,192},{192,224},{224... | collective-permute-start | bytes 884744 | tf_op jit(solution)/shard_map/cond/branch_0_fun/ppermute | solution.py:362
  43.0 4.5 %collective-permute-done.4 = f32[12,48,128]{2,1,0:T(8,128)S(1)} collective-permute-done((f32[12,48,128]{2,1,0:T(8,128)S(1)}, f32[12,48,128]{2,1,0:T(8,128)S(1)}, u32[]{:S(2)}, u32[]{:S(2)}) %collective-permute-start.4) | collective-permute-done | bytes 294944 | tf_op jit(solution)/shard_map/cond/branch_0_fun/ppermute | solution.py:362
  47.6 2.7 %collective-permute-start.11 = (f32[12,48,128]{2,1,0:T(8,128)S(1)}, f32[12,48,128]{2,1,0:T(8,128)}, u32[]{:S(2)}, u32[]{:S(2)}) collective-permute-start(f32[12,48,128]{2,1,0:T(8,128)S(1)} %collective-permute-done.10), channel_id=1, source_target_pairs={{0,224},{32,0},{64,32},{96,64},{128,96},{160,128},{192,160},{224,1... | collective-permute-start | bytes 884744 | tf_op jit(solution)/shard_map/cond/branch_0_fun/ppermute | solution.py:362
  50.2 3.0 %collective-permute-done.13 = f32[12,48,128]{2,1,0:T(8,128)} collective-permute-done((f32[12,48,128]{2,1,0:T(8,128)}, f32[12,48,128]{2,1,0:T(8,128)}, u32[]{:S(2)}, u32[]{:S(2)}) %collective-permute-start.13) | collective-permute-done | bytes 294944 | tf_op jit(solution)/shard_map/cond/branch_0_fun/ppermute | solution.py:362
  53.2 3.4 %collective-permute-start.14 = (f32[12,48,128]{2,1,0:T(8,128)}, f32[12,48,128]{2,1,0:T(8,128)}, u32[]{:S(2)}, u32[]{:S(2)}) collective-permute-start(f32[12,48,128]{2,1,0:T(8,128)} %collective-permute-done.13), channel_id=1, source_target_pairs={{0,224},{32,0},{64,32},{96,64},{128,96},{160,128},{192,160},{224,1... | collective-permute-start | bytes 884744 | tf_op jit(solution)/shard_map/cond/branch_0_fun/ppermute | solution.py:362
  56.7 3.5 %collective-permute-done.6 = f32[12,48,128]{2,1,0:T(8,128)S(1)} collective-permute-done((f32[12,48,128]{2,1,0:T(8,128)S(1)}, f32[12,48,128]{2,1,0:T(8,128)S(1)}, u32[]{:S(2)}, u32[]{:S(2)}) %collective-permute-start.6) | collective-permute-done | bytes 294944 | tf_op jit(solution)/shard_map/cond/branch_0_fun/ppermute | solution.py:362
  60.2 2.8 %collective-permute-start.12 = (f32[12,48,128]{2,1,0:T(8,128)}, f32[12,48,128]{2,1,0:T(8,128)}, u32[]{:S(2)}, u32[]{:S(2)}) collective-permute-start(f32[12,48,128]{2,1,0:T(8,128)} %collective-permute-done.11), channel_id=1, source_target_pairs={{0,224},{32,0},{64,32},{96,64},{128,96},{160,128},{192,160},{224,1... | collective-permute-start | bytes 884744 | tf_op jit(solution)/shard_map/cond/branch_0_fun/ppermute | solution.py:362
  64.1 1.7 %collective-permute-done.14 = f32[12,48,128]{2,1,0:T(8,128)} collective-permute-done((f32[12,48,128]{2,1,0:T(8,128)}, f32[12,48,128]{2,1,0:T(8,128)}, u32[]{:S(2)}, u32[]{:S(2)}) %collective-permute-start.14) | collective-permute-done | bytes 294944 | tf_op jit(solution)/shard_map/cond/branch_0_fun/ppermute | solution.py:362
  65.9 4.1 %collective-permute-done.8 = f32[12,48,128]{2,1,0:T(8,128)} collective-permute-done((f32[12,48,128]{2,1,0:T(8,128)S(1)}, f32[12,48,128]{2,1,0:T(8,128)}, u32[]{:S(2)}, u32[]{:S(2)}) %collective-permute-start.8) | collective-permute-done | bytes 294944 | tf_op jit(solution)/shard_map/cond/branch_0_fun/ppermute | solution.py:362
  70.0 2.2 %collective-permute-done.12 = f32[12,48,128]{2,1,0:T(8,128)} collective-permute-done((f32[12,48,128]{2,1,0:T(8,128)}, f32[12,48,128]{2,1,0:T(8,128)}, u32[]{:S(2)}, u32[]{:S(2)}) %collective-permute-start.12) | collective-permute-done | bytes 294944 | tf_op jit(solution)/shard_map/cond/branch_0_fun/ppermute | solution.py:362
  72.2 1.6 %copy-done.6 = f32[32,192,128]{2,1,0:T(8,128)} copy-done((f32[32,192,128]{2,1,0:T(8,128)}, f32[32,192,128]{2,1,0:T(8,128)S(1)}, u32[]{:S(2)}) %copy-start.6) | copy-done | bytes 3145752 | tf_op jit(solution)/shard_map/cond
  73.8 11.5 %branch_0_fun.6 = f32[2,16,24,128]{3,2,1,0:T(8,128)} custom-call(s32[6]{0:T(128)S(1)} %copy-done.10, s32[2,1,256]{2,1,0:T(1,128)} %broadcast_xor_fusion.labels_ref, f32[16,2,12,16,128]{4,3,2,1,0:T(8,128)} %bitcast.64, f32[1,12,48,128]{3,2,1,0:T(8,128)} %bitcast.59, f32[1,12,48,128]{3,2,1,0:T(8,128)} %bitcast.74, f32[1,12,48,128]{3,2,1,0:T(8,128)} %bitcast.72, ...), custom_call_target="tpu_custom_call" | custom-call | flops 3623878656 | bytes 10000000 | tf_op jit(solution)/shard_map/cond/branch_0_fun/pallas_call | solution.py:272
  85.4 19.6 %all_to_all.29.parts_ref = f32[32,24,128]{2,1,0:T(8,128)S(1)} all-to-all(f32[32,24,128]{2,1,0:T(8,128)} %bitcast.70), channel_id=1, replica_groups=mesh['z'=8,'yl'=2,'ja'=16] {'yl','ja'}, dimensions={0} | all-to-all | bytes 786432 | tf_op jit(solution)/shard_map/cond/branch_0_fun/all_to_all | solution.py:377
  105.0 1.6 %branch_0_fun.7 = f32[256,128]{1,0:T(8,128)} custom-call(s32[6]{0:T(128)S(1)} %copy-done.10, s32[2,1,256]{2,1,0:T(1,128)S(1)} %copy-done.3, f32[32,24,128]{2,1,0:T(8,128)S(1)} %all_to_all.29.parts_ref), custom_call_target="tpu_custom_call" | custom-call | tf_op jit(solution)/shard_map/cond/branch_0_fun/pallas_call | solution.py:309
  106.6 5.0 %all-to-all-start.6 = ((f32[16,16,128]{2,1,0:T(8,128)}), f32[16,16,128]{2,1,0:T(8,128)S(1)}, u32[]{:S(2)}, u32[]{:S(2)}) async-start(f32[16,16,128]{2,1,0:T(8,128)} %bitcast.38), calls=%async_computation.6 | async-start | bytes 262144 | tf_op jit(solution)/shard_map/all_to_all | solution.py:320
  111.7 0.7 dynamic_slice.15
  113.2 7.2 %all-to-all-done.6 = f32[16,16,128]{2,1,0:T(8,128)S(1)} async-done(((f32[16,16,128]{2,1,0:T(8,128)}), f32[16,16,128]{2,1,0:T(8,128)S(1)}, u32[]{:S(2)}, u32[]{:S(2)}) %all-to-all-start.6) | async-done | bytes 131104 | tf_op jit(solution)/shard_map/all_to_all | solution.py:320
  120.4 1.0 fusion
  121.5 0.7 copy.19
  (56 shorter events, 2.3 us)
Async XLA Ops:
  2.0 109.5 %copy-start.16 = (f32[384]{0:T(512)S(1)}, f32[384]{0:T(512)}, u32[]{:S(2)}) copy-start(f32[384]{0:T(512)} %param.16) | copy-start | bytes 4612
  2.1 109.5 %slice-start = ((f32[384]{0:T(512)}), f32[2]{0:T(128)S(1)}, s32[]{:S(2)}) async-start(f32[384]{0:T(512)} %param.16), calls=%async_computation.7 | async-start | bytes 1024 | tf_op jit(solution)/shard_map/slice | solution.py:323
  2.1 10.6 %copy-start.10 = (s32[6]{0:T(128)S(1)}, s32[6]{0:T(128)}, u32[]{:S(2)}) copy-start(s32[6]{0:T(128)} %get-tuple-element.106.vir) | copy-start | bytes 76 | tf_op jit(solution)/shard_map/cond
  2.1 10.6 %copy-start.13 = (s32[64]{0:T(128)S(1)}, s32[64]{0:T(128)}, u32[]{:S(2)}) copy-start(s32[64]{0:T(128)} %get-tuple-element.107.occ) | copy-start | bytes 772 | tf_op jit(solution)/shard_map/cond
  4.8 15.7 %copy-start.5 = (f32[12,48,128]{2,1,0:T(8,128)}, f32[12,48,128]{2,1,0:T(8,128)S(1)}, u32[]{:S(2)}) copy-start(f32[12,48,128]{2,1,0:T(8,128)S(1)} %get-tuple-element.111) | copy-start | bytes 884740 | tf_op jit(solution)/shard_map/cond
  4.8 15.7 %collective-permute-start.1 = (f32[12,48,128]{2,1,0:T(8,128)S(1)}, f32[12,48,128]{2,1,0:T(8,128)S(1)}, u32[]{:S(2)}, u32[]{:S(2)}) collective-permute-start(f32[12,48,128]{2,1,0:T(8,128)S(1)} %get-tuple-element.111), channel_id=1, source_target_pairs={{0,32},{32,64},{64,96},{96,128},{128,160},{160,192},{192,224},{224... | collective-permute-start | bytes 884744 | tf_op jit(solution)/shard_map/cond/branch_0_fun/ppermute | solution.py:362
  7.4 13.1 %collective-permute-start.2 = (f32[12,48,128]{2,1,0:T(8,128)S(1)}, f32[12,48,128]{2,1,0:T(8,128)S(1)}, u32[]{:S(2)}, u32[]{:S(2)}) collective-permute-start(f32[12,48,128]{2,1,0:T(8,128)S(1)} %get-tuple-element.111), channel_id=1, source_target_pairs={{0,224},{32,0},{64,32},{96,64},{128,96},{160,128},{192,160},{224,1... | collective-permute-start | bytes 884744 | tf_op jit(solution)/shard_map/cond/branch_0_fun/ppermute | solution.py:362
  11.4 9.1 %collective-permute-start = (f32[12,48,128]{2,1,0:T(8,128)S(1)}, f32[12,48,128]{2,1,0:T(8,128)S(1)}, u32[]{:S(2)}, u32[]{:S(2)}) collective-permute-start(f32[12,48,128]{2,1,0:T(8,128)S(1)} %get-tuple-element.110), channel_id=1, source_target_pairs={{0,16},{16,0},{1,17},{17,1},{2,18},{18,2},{3,19},{19,3},{4,20},{20... | collective-permute-start | bytes 884744 | tf_op jit(solution)/shard_map/cond/branch_0_fun/ppermute | solution.py:334
  20.5 11.3 %copy-start.22 = (f32[12,48,128]{2,1,0:T(8,128)}, f32[12,48,128]{2,1,0:T(8,128)S(1)}, u32[]{:S(2)}) copy-start(f32[12,48,128]{2,1,0:T(8,128)S(1)} %collective-permute-done.1) | copy-start | bytes 884740 | tf_op jit(solution)/shard_map/cond
  20.5 0.8 copy-start.23
  21.3 0.7 copy-start.24
  22.0 50.2 %all-to-all-start = ((f32[32,192,128]{2,1,0:T(8,128)}), f32[32,192,128]{2,1,0:T(8,128)S(1)}, u32[]{:S(2)}, u32[]{:S(2)}) async-start(f32[32,192,128]{2,1,0:T(8,128)} %bitcast.1), calls=%async_computation | async-start | bytes 6291456 | tf_op jit(solution)/shard_map/cond/branch_0_fun/all_to_all | solution.py:371
  30.0 8.7 %collective-permute-start.9 = (f32[12,48,128]{2,1,0:T(8,128)}, f32[12,48,128]{2,1,0:T(8,128)S(1)}, u32[]{:S(2)}, u32[]{:S(2)}) collective-permute-start(f32[12,48,128]{2,1,0:T(8,128)} %copy-done.24), channel_id=1, source_target_pairs={{0,224},{32,0},{64,32},{96,64},{128,96},{160,128},{192,160},{224,1... | collective-permute-start | bytes 884744 | tf_op jit(solution)/shard_map/cond/branch_0_fun/ppermute | solution.py:362
  31.8 9.8 %collective-permute-start.3 = (f32[12,48,128]{2,1,0:T(8,128)}, f32[12,48,128]{2,1,0:T(8,128)S(1)}, u32[]{:S(2)}, u32[]{:S(2)}) collective-permute-start(f32[12,48,128]{2,1,0:T(8,128)} %copy-done.24), channel_id=1, source_target_pairs={{0,32},{32,64},{64,96},{96,128},{128,160},{160,192},{192,224},{224... | collective-permute-start | bytes 884744 | tf_op jit(solution)/shard_map/cond/branch_0_fun/ppermute | solution.py:362
  31.8 15.8 %collective-permute-start.4 = (f32[12,48,128]{2,1,0:T(8,128)S(1)}, f32[12,48,128]{2,1,0:T(8,128)S(1)}, u32[]{:S(2)}, u32[]{:S(2)}) collective-permute-start(f32[12,48,128]{2,1,0:T(8,128)S(1)} %collective-permute-done.1), channel_id=1, source_target_pairs={{0,32},{32,64},{64,96},{96,128},{128,160},{160,192},{192,224},{224... | collective-permute-start | bytes 884744 | tf_op jit(solution)/shard_map/cond/branch_0_fun/ppermute | solution.py:362
  38.7 24.3 %copy-start.25 = (f32[12,48,128]{2,1,0:T(8,128)}, f32[12,48,128]{2,1,0:T(8,128)S(1)}, u32[]{:S(2)}) copy-start(f32[12,48,128]{2,1,0:T(8,128)S(1)} %collective-permute-done.9) | copy-start | bytes 884740 | tf_op jit(solution)/shard_map/cond
  38.7 8.9 %collective-permute-start.10 = (f32[12,48,128]{2,1,0:T(8,128)S(1)}, f32[12,48,128]{2,1,0:T(8,128)S(1)}, u32[]{:S(2)}, u32[]{:S(2)}) collective-permute-start(f32[12,48,128]{2,1,0:T(8,128)S(1)} %collective-permute-done.9), channel_id=1, source_target_pairs={{0,224},{32,0},{64,32},{96,64},{128,96},{160,128},{192,160},{224,1... | collective-permute-start | bytes 884744 | tf_op jit(solution)/shard_map/cond/branch_0_fun/ppermute | solution.py:362
  41.6 11.7 %collective-permute-start.13 = (f32[12,48,128]{2,1,0:T(8,128)}, f32[12,48,128]{2,1,0:T(8,128)}, u32[]{:S(2)}, u32[]{:S(2)}) collective-permute-start(f32[12,48,128]{2,1,0:T(8,128)} %copy-done.23), channel_id=1, source_target_pairs={{0,224},{32,0},{64,32},{96,64},{128,96},{160,128},{192,160},{224,1... | collective-permute-start | bytes 884744 | tf_op jit(solution)/shard_map/cond/branch_0_fun/ppermute | solution.py:362
  41.6 21.4 %copy-start.26 = (f32[12,48,128]{2,1,0:T(8,128)}, f32[12,48,128]{2,1,0:T(8,128)S(1)}, u32[]{:S(2)}) copy-start(f32[12,48,128]{2,1,0:T(8,128)S(1)} %collective-permute-done.3) | copy-start | bytes 884740 | tf_op jit(solution)/shard_map/cond
  41.6 15.1 %collective-permute-start.5 = (f32[12,48,128]{2,1,0:T(8,128)S(1)}, f32[12,48,128]{2,1,0:T(8,128)}, u32[]{:S(2)}, u32[]{:S(2)}) collective-permute-start(f32[12,48,128]{2,1,0:T(8,128)S(1)} %collective-permute-done.3), channel_id=1, source_target_pairs={{0,32},{32,64},{64,96},{96,128},{128,160},{160,192},{192,224},{224... | collective-permute-start | bytes 884744 | tf_op jit(solution)/shard_map/cond/branch_0_fun/ppermute | solution.py:362
  47.6 15.4 %copy-start.27 = (f32[12,48,128]{2,1,0:T(8,128)}, f32[12,48,128]{2,1,0:T(8,128)S(1)}, u32[]{:S(2)}) copy-start(f32[12,48,128]{2,1,0:T(8,128)S(1)} %collective-permute-done.4) | copy-start | bytes 884740 | tf_op jit(solution)/shard_map/cond
  47.6 12.6 %collective-permute-start.6 = (f32[12,48,128]{2,1,0:T(8,128)S(1)}, f32[12,48,128]{2,1,0:T(8,128)S(1)}, u32[]{:S(2)}, u32[]{:S(2)}) collective-permute-start(f32[12,48,128]{2,1,0:T(8,128)S(1)} %collective-permute-done.4), channel_id=1, source_target_pairs={{0,32},{32,64},{64,96},{96,128},{128,160},{160,192},{192,224},{224... | collective-permute-start | bytes 884744 | tf_op jit(solution)/shard_map/cond/branch_0_fun/ppermute | solution.py:362
  47.6 15.4 %copy-start.28 = (f32[12,48,128]{2,1,0:T(8,128)}, f32[12,48,128]{2,1,0:T(8,128)S(1)}, u32[]{:S(2)}) copy-start(f32[12,48,128]{2,1,0:T(8,128)S(1)} %collective-permute-done.10) | copy-start | bytes 884740 | tf_op jit(solution)/shard_map/cond
  47.6 12.6 %collective-permute-start.11 = (f32[12,48,128]{2,1,0:T(8,128)S(1)}, f32[12,48,128]{2,1,0:T(8,128)}, u32[]{:S(2)}, u32[]{:S(2)}) collective-permute-start(f32[12,48,128]{2,1,0:T(8,128)S(1)} %collective-permute-done.10), channel_id=1, source_target_pairs={{0,224},{32,0},{64,32},{96,64},{128,96},{160,128},{192,160},{224,1... | collective-permute-start | bytes 884744 | tf_op jit(solution)/shard_map/cond/branch_0_fun/ppermute | solution.py:362
  53.2 12.6 %collective-permute-start.14 = (f32[12,48,128]{2,1,0:T(8,128)}, f32[12,48,128]{2,1,0:T(8,128)}, u32[]{:S(2)}, u32[]{:S(2)}) collective-permute-start(f32[12,48,128]{2,1,0:T(8,128)} %collective-permute-done.13), channel_id=1, source_target_pairs={{0,224},{32,0},{64,32},{96,64},{128,96},{160,128},{192,160},{224,1... | collective-permute-start | bytes 884744 | tf_op jit(solution)/shard_map/cond/branch_0_fun/ppermute | solution.py:362
  56.6 9.2 %collective-permute-start.7 = (f32[12,48,128]{2,1,0:T(8,128)}, f32[12,48,128]{2,1,0:T(8,128)}, u32[]{:S(2)}, u32[]{:S(2)}) collective-permute-start(f32[12,48,128]{2,1,0:T(8,128)} %collective-permute-done.5), channel_id=1, source_target_pairs={{0,32},{32,64},{64,96},{96,128},{128,160},{160,192},{192,224},{224... | collective-permute-start | bytes 884744 | tf_op jit(solution)/shard_map/cond/branch_0_fun/ppermute | solution.py:362
  60.2 12.0 %copy-start.29 = (f32[12,48,128]{2,1,0:T(8,128)}, f32[12,48,128]{2,1,0:T(8,128)S(1)}, u32[]{:S(2)}) copy-start(f32[12,48,128]{2,1,0:T(8,128)S(1)} %collective-permute-done.6) | copy-start | bytes 884740 | tf_op jit(solution)/shard_map/cond
  60.2 9.8 %collective-permute-start.8 = (f32[12,48,128]{2,1,0:T(8,128)S(1)}, f32[12,48,128]{2,1,0:T(8,128)}, u32[]{:S(2)}, u32[]{:S(2)}) collective-permute-start(f32[12,48,128]{2,1,0:T(8,128)S(1)} %collective-permute-done.6), channel_id=1, source_target_pairs={{0,32},{32,64},{64,96},{96,128},{128,160},{160,192},{192,224},{224... | collective-permute-start | bytes 884744 | tf_op jit(solution)/shard_map/cond/branch_0_fun/ppermute | solution.py:362
  60.2 12.0 %collective-permute-start.12 = (f32[12,48,128]{2,1,0:T(8,128)}, f32[12,48,128]{2,1,0:T(8,128)}, u32[]{:S(2)}, u32[]{:S(2)}) collective-permute-start(f32[12,48,128]{2,1,0:T(8,128)} %collective-permute-done.11), channel_id=1, source_target_pairs={{0,224},{32,0},{64,32},{96,64},{128,96},{160,128},{192,160},{224,1... | collective-permute-start | bytes 884744 | tf_op jit(solution)/shard_map/cond/branch_0_fun/ppermute | solution.py:362
  72.2 1.6 %copy-start.6 = (f32[32,192,128]{2,1,0:T(8,128)}, f32[32,192,128]{2,1,0:T(8,128)S(1)}, u32[]{:S(2)}) copy-start(f32[32,192,128]{2,1,0:T(8,128)S(1)} %all-to-all-done) | copy-start | bytes 9437188 | tf_op jit(solution)/shard_map/cond
  73.8 31.1 %copy-start.3 = (s32[2,1,256]{2,1,0:T(1,128)S(1)}, s32[2,1,256]{2,1,0:T(1,128)}, u32[]{:S(2)}) copy-start(s32[2,1,256]{2,1,0:T(1,128)} %broadcast_xor_fusion.labels_ref) | copy-start | bytes 6148 | tf_op jit(solution)/shard_map/cond
  106.6 13.8 %all-to-all-start.6 = ((f32[16,16,128]{2,1,0:T(8,128)}), f32[16,16,128]{2,1,0:T(8,128)S(1)}, u32[]{:S(2)}, u32[]{:S(2)}) async-start(f32[16,16,128]{2,1,0:T(8,128)} %bitcast.38), calls=%async_computation.6 | async-start | bytes 262144 | tf_op jit(solution)/shard_map/all_to_all | solution.py:320
where the time goes:
time: 123 us; the launch traced here: 122 us
  starting transfers between devices  35.8 us (29%)
  waiting for transfers between devices  33.3 us (27%)
  Pallas kernels  25 us (20%)
  blocking collectives  19.6 us (16%)
  local copies, waits for them, and re-layouts  5.29 us (4%)
  other arithmetic  2.44 us (2%)
    ppermute x14, waiting for transfers between devices, hop(): lax.ppermute(ring[other, behind - side], 'z', forward if side > 0 else ba...  26 us
    ppermute x14, starting transfers between devices, hop(): lax.ppermute(ring[other, behind - side], 'z', forward if side > 0 else ba...  21.5 us
    all_to_all x1, blocking collectives, ladder_rows(): lax.all_to_all(parts.reshape((YL * JA,) + parts.shape[2:]), ('yl', 'ja'),...  19.6 us
    pallas_call x1, Pallas kernels, contract(): pl.pallas_call(functools.partial(contract_kernel, keep_all), out_shape=ja...  11.5 us
    all_to_all x1, starting transfers between devices, ladder_rows(): lax.all_to_all(packed.reshape(JA * YL, lane_tiles(slots) * PAIRS, LANES),...  8.03 us
    pallas_call x1, Pallas kernels, pack_amplitudes(): pl.pallas_call(functools.partial(pack_amplitudes_kernel, slots), out_shap...  7.76 us
    all_to_all x1, waiting for transfers between devices, finish(): lax.all_to_all(ladder, ('z', 'yl'), split_axis=0, concat_axis=0, tiled=True)  7.23 us
    all_to_all x1, starting transfers between devices, finish(): lax.all_to_all(ladder, ('z', 'yl'), split_axis=0, concat_axis=0, tiled=True)  4.98 us
  transfers between devices with their start and end apart: 17, of which 8 were waited for; matrix products, arithmetic and copies ran while one was open for 2% of the time, Pallas kernels for 6%

commit v1 on v0

--- a/solution.py
+++ b/solution.py
@@ -364,7 +364,7 @@
         for of in HOPS[:2]:
             hop(*of)
         packed = pack_amplitudes(amplitudes, occ_irrep, vir_irrep, slots)
-        packed, ring[1, 0], ring[0, 1], ring[0, -1] = lax.optimization_barrier((packed, ring[1, 0], ring[0, 1], ring[0, -1]))
+        packed, ring[1, 0], ring[0, 1] = lax.optimization_barrier((packed, ring[1, 0], ring[0, 1]))
         for of in HOPS[2:]:
             hop(*of)
         ring = [ring[key][None] for key in RING]

time: 123 us -> 125 us (1.016)
  waiting for transfers between devices: 33.3 us -> 35.3 us
  starting transfers between devices: 35.8 us -> 37.3 us
    ppermute x14, waiting for transfers between devices: 26 us -> 28.1 us  [hop(): lax.ppermute(ring[other, behind - side], 'z', forward if side > 0 else ba...]
    cond x26 -> x24, local copies, waits for them, and re-layouts: 3.14 us -> 2.49 us
  transfers between devices with their start and end apart: 17 -> 17, of which waited for: 8 -> 12; matrix products, arithmetic and copies ran while one was open for 2% -> 2% of each run, Pallas kernels for 6% -> 6%
where the time goes in v1:
time: 125 us; the launch traced here: 124 us
  starting transfers between devices  37.3 us (30%)
  waiting for transfers between devices  35.3 us (28%)
  Pallas kernels  25 us (20%)
  blocking collectives  18.7 us (15%)
  local copies, waits for them, and re-layouts  4.64 us (4%)
  other arithmetic  2.44 us (2%)
    ppermute x14, waiting for transfers between devices, hop(): lax.ppermute(ring[other, behind - side], 'z', forward if side > 0 else ba...  28.1 us
    ppermute x14, starting transfers between devices, hop(): lax.ppermute(ring[other, behind - side], 'z', forward if side > 0 else ba...  21.5 us
    all_to_all x1, blocking collectives, ladder_rows(): lax.all_to_all(parts.reshape((YL * JA,) + parts.shape[2:]), ('yl', 'ja'),...  18.7 us
    pallas_call x1, Pallas kernels, contract(): pl.pallas_call(functools.partial(contract_kernel, keep_all), out_shape=ja...  11.5 us
    all_to_all x1, starting transfers between devices, ladder_rows(): lax.all_to_all(packed.reshape(JA * YL, lane_tiles(slots) * PAIRS, LANES),...  8.31 us
    pallas_call x1, Pallas kernels, pack_amplitudes(): pl.pallas_call(functools.partial(pack_amplitudes_kernel, slots), out_shap...  7.75 us
    all_to_all x1, waiting for transfers between devices, finish(): lax.all_to_all(ladder, ('z', 'yl'), split_axis=0, concat_axis=0, tiled=True)  7.23 us
    all_to_all x1, starting transfers between devices, finish(): lax.all_to_all(ladder, ('z', 'yl'), split_axis=0, concat_axis=0, tiled=True)  6.12 us
  transfers between devices with their start and end apart: 17, of which 12 were waited for; matrix products, arithmetic and copies ran while one was open for 2% of the time, Pallas kernels for 6%

profile of v1, /device:TPU:1, one launch (start us, length us, event | category | flops | bytes accessed | tf_op | source)
XLA Modules:
  0.0 124.2 jit_solution(1260490492854854324)
XLA Ops:
  0.0 1.4 %shard_map.64 = s32[1]{0:T(128)} custom-call(s32[64]{0:T(128)} %occ.1, s32[6]{0:T(128)} %vir.1), custom_call_target="tpu_custom_call" | custom-call | tf_op jit(solution)/shard_map/pallas_call | solution.py:401
  2.1 105.3 %conditional.1 = (f32[256,128]{1,0:T(8,128)}) conditional(s32[]{:T(128)} %bitcast.35, (s32[64]{0:T(128)}, f32[4,4,384,384]{3,2,1,0:T(8,128)}, s32[6]{0:T(128)}, f32[48,24,384]{2,1,0:T(8,128)}) %tuple.31, (s32[64]{0:T(128)}, f32[4,4,384,384]{3,2,1,0:T(8,128)}, s32[6]{0:T(128)}, f32[48,24,384]{2,1,0:T(8,128)}) %tuple.31, (s32[6]{0:T(128)}, ...), branch_computations={%region_0.0_spmd, %region_1.0_spmd, %region_2.5_spmd} | conditional | flops 10883079168 | bytes 151084832 | solution.py:405
  2.1 2.7 %branch_0_fun.5 = (f32[12,48,128]{2,1,0:T(8,128)S(1)}, f32[12,48,128]{2,1,0:T(8,128)S(1)}) custom-call(s32[6]{0:T(128)} %get-tuple-element.106.vir, f32[48,24,384]{2,1,0:T(8,128)} %get-tuple-element.109.v_ref), custom_call_target="tpu_custom_call" | custom-call | flops 1000000 | bytes 3000000 | tf_op jit(solution)/shard_map/cond/branch_0_fun/pallas_call | solution.py:153
  4.8 2.5 %collective-permute-start.1 = (f32[12,48,128]{2,1,0:T(8,128)S(1)}, f32[12,48,128]{2,1,0:T(8,128)S(1)}, u32[]{:S(2)}, u32[]{:S(2)}) collective-permute-start(f32[12,48,128]{2,1,0:T(8,128)S(1)} %get-tuple-element.111), channel_id=1, source_target_pairs={{0,32},{32,64},{64,96},{96,128},{128,160},{160,192},{192,224},{224... | collective-permute-start | bytes 884744 | tf_op jit(solution)/shard_map/cond/branch_0_fun/ppermute | solution.py:362
  7.4 1.3 %collective-permute-start = (f32[12,48,128]{2,1,0:T(8,128)S(1)}, f32[12,48,128]{2,1,0:T(8,128)S(1)}, u32[]{:S(2)}, u32[]{:S(2)}) collective-permute-start(f32[12,48,128]{2,1,0:T(8,128)S(1)} %get-tuple-element.110), channel_id=1, source_target_pairs={{0,16},{16,0},{1,17},{17,1},{2,18},{18,2},{3,19},{19,3},{4,20},{20... | collective-permute-start | bytes 884744 | tf_op jit(solution)/shard_map/cond/branch_0_fun/ppermute | solution.py:334
  8.7 7.8 %branch_0_fun.4 = f32[16,384,128]{2,1,0:T(8,128)} custom-call(s32[64]{0:T(128)S(1)} %copy-done.13, s32[6]{0:T(128)S(1)} %copy-done.10, f32[16,384,384]{2,1,0:T(8,128)} %bitcast.60), custom_call_target="tpu_custom_call" | custom-call | flops 10000000 | bytes 14000000 | tf_op jit(solution)/shard_map/cond/branch_0_fun/pallas_call | solution.py:122
  16.4 1.6 %collective-permute-done.1 = f32[12,48,128]{2,1,0:T(8,128)S(1)} collective-permute-done((f32[12,48,128]{2,1,0:T(8,128)S(1)}, f32[12,48,128]{2,1,0:T(8,128)S(1)}, u32[]{:S(2)}, u32[]{:S(2)}) %collective-permute-start.1) | collective-permute-done | bytes 294944 | tf_op jit(solution)/shard_map/cond/branch_0_fun/ppermute | solution.py:362
  18.9 8.3 %all-to-all-start = ((f32[32,192,128]{2,1,0:T(8,128)}), f32[32,192,128]{2,1,0:T(8,128)S(1)}, u32[]{:S(2)}, u32[]{:S(2)}) async-start(f32[32,192,128]{2,1,0:T(8,128)} %bitcast.1), calls=%async_computation | async-start | bytes 6291456 | tf_op jit(solution)/shard_map/cond/branch_0_fun/all_to_all | solution.py:371
  27.2 1.9 %collective-permute-start.8 = (f32[12,48,128]{2,1,0:T(8,128)}, f32[12,48,128]{2,1,0:T(8,128)S(1)}, u32[]{:S(2)}, u32[]{:S(2)}) collective-permute-start(f32[12,48,128]{2,1,0:T(8,128)} %copy-done.23), channel_id=1, source_target_pairs={{0,224},{32,0},{64,32},{96,64},{128,96},{160,128},{192,160},{224,1... | collective-permute-start | bytes 884744 | tf_op jit(solution)/shard_map/cond/branch_0_fun/ppermute | solution.py:362
  29.1 1.6 %collective-permute-start.12 = (f32[12,48,128]{2,1,0:T(8,128)S(1)}, f32[12,48,128]{2,1,0:T(8,128)S(1)}, u32[]{:S(2)}, u32[]{:S(2)}) collective-permute-start(f32[12,48,128]{2,1,0:T(8,128)S(1)} %get-tuple-element.111), channel_id=1, source_target_pairs={{0,224},{32,0},{64,32},{96,64},{128,96},{160,128},{192,160},{224,1... | collective-permute-start | bytes 884744 | tf_op jit(solution)/shard_map/cond/branch_0_fun/ppermute | solution.py:362
  30.8 5.1 %collective-permute-done.8 = f32[12,48,128]{2,1,0:T(8,128)S(1)} collective-permute-done((f32[12,48,128]{2,1,0:T(8,128)}, f32[12,48,128]{2,1,0:T(8,128)S(1)}, u32[]{:S(2)}, u32[]{:S(2)}) %collective-permute-start.8) | collective-permute-done | bytes 294944 | tf_op jit(solution)/shard_map/cond/branch_0_fun/ppermute | solution.py:362
  35.9 3.1 %collective-permute-start.9 = (f32[12,48,128]{2,1,0:T(8,128)S(1)}, f32[12,48,128]{2,1,0:T(8,128)S(1)}, u32[]{:S(2)}, u32[]{:S(2)}) collective-permute-start(f32[12,48,128]{2,1,0:T(8,128)S(1)} %collective-permute-done.8), channel_id=1, source_target_pairs={{0,224},{32,0},{64,32},{96,64},{128,96},{160,128},{192,160},{224,1... | collective-permute-start | bytes 884744 | tf_op jit(solution)/shard_map/cond/branch_0_fun/ppermute | solution.py:362
  38.9 3.2 %collective-permute-done.12 = f32[12,48,128]{2,1,0:T(8,128)S(1)} collective-permute-done((f32[12,48,128]{2,1,0:T(8,128)S(1)}, f32[12,48,128]{2,1,0:T(8,128)S(1)}, u32[]{:S(2)}, u32[]{:S(2)}) %collective-permute-start.12) | collective-permute-done | bytes 294944 | tf_op jit(solution)/shard_map/cond/branch_0_fun/ppermute | solution.py:362
  42.2 3.1 %collective-permute-start.13 = (f32[12,48,128]{2,1,0:T(8,128)S(1)}, f32[12,48,128]{2,1,0:T(8,128)}, u32[]{:S(2)}, u32[]{:S(2)}) collective-permute-start(f32[12,48,128]{2,1,0:T(8,128)S(1)} %collective-permute-done.12), channel_id=1, source_target_pairs={{0,224},{32,0},{64,32},{96,64},{128,96},{160,128},{192,160},{224,1... | collective-permute-start | bytes 884744 | tf_op jit(solution)/shard_map/cond/branch_0_fun/ppermute | solution.py:362
  45.3 1.0 collective-permute-done.3
  46.3 2.2 %collective-permute-done.9 = f32[12,48,128]{2,1,0:T(8,128)S(1)} collective-permute-done((f32[12,48,128]{2,1,0:T(8,128)S(1)}, f32[12,48,128]{2,1,0:T(8,128)S(1)}, u32[]{:S(2)}, u32[]{:S(2)}) %collective-permute-start.9) | collective-permute-done | bytes 294944 | tf_op jit(solution)/shard_map/cond/branch_0_fun/ppermute | solution.py:362
  48.5 3.1 %collective-permute-start.10 = (f32[12,48,128]{2,1,0:T(8,128)S(1)}, f32[12,48,128]{2,1,0:T(8,128)}, u32[]{:S(2)}, u32[]{:S(2)}) collective-permute-start(f32[12,48,128]{2,1,0:T(8,128)S(1)} %collective-permute-done.9), channel_id=1, source_target_pairs={{0,224},{32,0},{64,32},{96,64},{128,96},{160,128},{192,160},{224,1... | collective-permute-start | bytes 884744 | tf_op jit(solution)/shard_map/cond/branch_0_fun/ppermute | solution.py:362
  51.6 3.3 %collective-permute-done.13 = f32[12,48,128]{2,1,0:T(8,128)} collective-permute-done((f32[12,48,128]{2,1,0:T(8,128)S(1)}, f32[12,48,128]{2,1,0:T(8,128)}, u32[]{:S(2)}, u32[]{:S(2)}) %collective-permute-start.13) | collective-permute-done | bytes 294944 | tf_op jit(solution)/shard_map/cond/branch_0_fun/ppermute | solution.py:362
  54.9 3.1 %collective-permute-start.14 = (f32[12,48,128]{2,1,0:T(8,128)}, f32[12,48,128]{2,1,0:T(8,128)}, u32[]{:S(2)}, u32[]{:S(2)}) collective-permute-start(f32[12,48,128]{2,1,0:T(8,128)} %collective-permute-done.13), channel_id=1, source_target_pairs={{0,224},{32,0},{64,32},{96,64},{128,96},{160,128},{192,160},{224,1... | collective-permute-start | bytes 884744 | tf_op jit(solution)/shard_map/cond/branch_0_fun/ppermute | solution.py:362
  58.0 1.4 %collective-permute-done.5 = f32[12,48,128]{2,1,0:T(8,128)} collective-permute-done((f32[12,48,128]{2,1,0:T(8,128)S(1)}, f32[12,48,128]{2,1,0:T(8,128)}, u32[]{:S(2)}, u32[]{:S(2)}) %collective-permute-start.5) | collective-permute-done | bytes 294944 | tf_op jit(solution)/shard_map/cond/branch_0_fun/ppermute | solution.py:362
  59.4 1.8 %collective-permute-done.10 = f32[12,48,128]{2,1,0:T(8,128)} collective-permute-done((f32[12,48,128]{2,1,0:T(8,128)S(1)}, f32[12,48,128]{2,1,0:T(8,128)}, u32[]{:S(2)}, u32[]{:S(2)}) %collective-permute-start.10) | collective-permute-done | bytes 294944 | tf_op jit(solution)/shard_map/cond/branch_0_fun/ppermute | solution.py:362
  61.3 3.1 %collective-permute-start.11 = (f32[12,48,128]{2,1,0:T(8,128)}, f32[12,48,128]{2,1,0:T(8,128)}, u32[]{:S(2)}, u32[]{:S(2)}) collective-permute-start(f32[12,48,128]{2,1,0:T(8,128)} %collective-permute-done.10), channel_id=1, source_target_pairs={{0,224},{32,0},{64,32},{96,64},{128,96},{160,128},{192,160},{224,1... | collective-permute-start | bytes 884744 | tf_op jit(solution)/shard_map/cond/branch_0_fun/ppermute | solution.py:362
  65.5 2.1 %collective-permute-done.14 = f32[12,48,128]{2,1,0:T(8,128)} collective-permute-done((f32[12,48,128]{2,1,0:T(8,128)}, f32[12,48,128]{2,1,0:T(8,128)}, u32[]{:S(2)}, u32[]{:S(2)}) %collective-permute-start.14) | collective-permute-done | bytes 294944 | tf_op jit(solution)/shard_map/cond/branch_0_fun/ppermute | solution.py:362
  67.6 4.8 %collective-permute-done.7 = f32[12,48,128]{2,1,0:T(8,128)} collective-permute-done((f32[12,48,128]{2,1,0:T(8,128)}, f32[12,48,128]{2,1,0:T(8,128)}, u32[]{:S(2)}, u32[]{:S(2)}) %collective-permute-start.7) | collective-permute-done | bytes 294944 | tf_op jit(solution)/shard_map/cond/branch_0_fun/ppermute | solution.py:362
  72.4 1.5 %collective-permute-done.11 = f32[12,48,128]{2,1,0:T(8,128)} collective-permute-done((f32[12,48,128]{2,1,0:T(8,128)}, f32[12,48,128]{2,1,0:T(8,128)}, u32[]{:S(2)}, u32[]{:S(2)}) %collective-permute-start.11) | collective-permute-done | bytes 294944 | tf_op jit(solution)/shard_map/cond/branch_0_fun/ppermute | solution.py:362
  73.9 1.6 %copy-done.6 = f32[32,192,128]{2,1,0:T(8,128)} copy-done((f32[32,192,128]{2,1,0:T(8,128)}, f32[32,192,128]{2,1,0:T(8,128)S(1)}, u32[]{:S(2)}) %copy-start.6) | copy-done | bytes 3145752 | tf_op jit(solution)/shard_map/cond
  75.5 11.5 %branch_0_fun.6 = f32[2,16,24,128]{3,2,1,0:T(8,128)} custom-call(s32[6]{0:T(128)S(1)} %copy-done.10, s32[2,1,256]{2,1,0:T(1,128)} %broadcast_xor_fusion.labels_ref, f32[16,2,12,16,128]{4,3,2,1,0:T(8,128)} %bitcast.64, f32[1,12,48,128]{3,2,1,0:T(8,128)} %bitcast.59, f32[1,12,48,128]{3,2,1,0:T(8,128)} %bitcast.73, f32[1,12,48,128]{3,2,1,0:T(8,128)} %bitcast.72, ...), custom_call_target="tpu_custom_call" | custom-call | flops 3623878656 | bytes 10000000 | tf_op jit(solution)/shard_map/cond/branch_0_fun/pallas_call | solution.py:272
  87.0 18.7 %all_to_all.29.parts_ref = f32[32,24,128]{2,1,0:T(8,128)S(1)} all-to-all(f32[32,24,128]{2,1,0:T(8,128)} %bitcast.70), channel_id=1, replica_groups=mesh['z'=8,'yl'=2,'ja'=16] {'yl','ja'}, dimensions={0} | all-to-all | bytes 786432 | tf_op jit(solution)/shard_map/cond/branch_0_fun/all_to_all | solution.py:377
  105.8 1.6 %branch_0_fun.7 = f32[256,128]{1,0:T(8,128)} custom-call(s32[6]{0:T(128)S(1)} %copy-done.10, s32[2,1,256]{2,1,0:T(1,128)S(1)} %copy-done.3, f32[32,24,128]{2,1,0:T(8,128)S(1)} %all_to_all.29.parts_ref), custom_call_target="tpu_custom_call" | custom-call | tf_op jit(solution)/shard_map/cond/branch_0_fun/pallas_call | solution.py:309
  107.4 6.1 %all-to-all-start.6 = ((f32[16,16,128]{2,1,0:T(8,128)}), f32[16,16,128]{2,1,0:T(8,128)S(1)}, u32[]{:S(2)}, u32[]{:S(2)}) async-start(f32[16,16,128]{2,1,0:T(8,128)} %bitcast.38), calls=%async_computation.6 | async-start | bytes 262144 | tf_op jit(solution)/shard_map/all_to_all | solution.py:320
  115.2 7.2 %all-to-all-done.6 = f32[16,16,128]{2,1,0:T(8,128)S(1)} async-done(((f32[16,16,128]{2,1,0:T(8,128)}), f32[16,16,128]{2,1,0:T(8,128)S(1)}, u32[]{:S(2)}, u32[]{:S(2)}) %all-to-all-start.6) | async-done | bytes 131104 | tf_op jit(solution)/shard_map/all_to_all | solution.py:320
  122.4 1.0 fusion
  (54 shorter events, 4.5 us)
Async XLA Ops:
  2.0 111.5 %copy-start.16 = (f32[384]{0:T(512)S(1)}, f32[384]{0:T(512)}, u32[]{:S(2)}) copy-start(f32[384]{0:T(512)} %param.16) | copy-start | bytes 4612
  2.1 111.5 %slice-start = ((f32[384]{0:T(512)}), f32[2]{0:T(128)S(1)}, s32[]{:S(2)}) async-start(f32[384]{0:T(512)} %param.16), calls=%async_computation.7 | async-start | bytes 1024 | tf_op jit(solution)/shard_map/slice | solution.py:323
  2.1 6.6 %copy-start.10 = (s32[6]{0:T(128)S(1)}, s32[6]{0:T(128)}, u32[]{:S(2)}) copy-start(s32[6]{0:T(128)} %get-tuple-element.106.vir) | copy-start | bytes 76 | tf_op jit(solution)/shard_map/cond
  2.1 6.6 %copy-start.13 = (s32[64]{0:T(128)S(1)}, s32[64]{0:T(128)}, u32[]{:S(2)}) copy-start(s32[64]{0:T(128)} %get-tuple-element.107.occ) | copy-start | bytes 772 | tf_op jit(solution)/shard_map/cond
  4.8 24.3 %copy-start.5 = (f32[12,48,128]{2,1,0:T(8,128)}, f32[12,48,128]{2,1,0:T(8,128)S(1)}, u32[]{:S(2)}) copy-start(f32[12,48,128]{2,1,0:T(8,128)S(1)} %get-tuple-element.111) | copy-start | bytes 884740 | tf_op jit(solution)/shard_map/cond
  4.8 13.2 %collective-permute-start.1 = (f32[12,48,128]{2,1,0:T(8,128)S(1)}, f32[12,48,128]{2,1,0:T(8,128)S(1)}, u32[]{:S(2)}, u32[]{:S(2)}) collective-permute-start(f32[12,48,128]{2,1,0:T(8,128)S(1)} %get-tuple-element.111), channel_id=1, source_target_pairs={{0,32},{32,64},{64,96},{96,128},{128,160},{160,192},{192,224},{224... | collective-permute-start | bytes 884744 | tf_op jit(solution)/shard_map/cond/branch_0_fun/ppermute | solution.py:362
  7.4 10.7 %collective-permute-start = (f32[12,48,128]{2,1,0:T(8,128)S(1)}, f32[12,48,128]{2,1,0:T(8,128)S(1)}, u32[]{:S(2)}, u32[]{:S(2)}) collective-permute-start(f32[12,48,128]{2,1,0:T(8,128)S(1)} %get-tuple-element.110), channel_id=1, source_target_pairs={{0,16},{16,0},{1,17},{17,1},{2,18},{18,2},{3,19},{19,3},{4,20},{20... | collective-permute-start | bytes 884744 | tf_op jit(solution)/shard_map/cond/branch_0_fun/ppermute | solution.py:334
  18.0 0.7 copy-start.22
  18.1 0.8 copy-start.23
  18.9 55.0 %all-to-all-start = ((f32[32,192,128]{2,1,0:T(8,128)}), f32[32,192,128]{2,1,0:T(8,128)S(1)}, u32[]{:S(2)}, u32[]{:S(2)}) async-start(f32[32,192,128]{2,1,0:T(8,128)} %bitcast.1), calls=%async_computation | async-start | bytes 6291456 | tf_op jit(solution)/shard_map/cond/branch_0_fun/all_to_all | solution.py:371
  27.2 8.7 %collective-permute-start.8 = (f32[12,48,128]{2,1,0:T(8,128)}, f32[12,48,128]{2,1,0:T(8,128)S(1)}, u32[]{:S(2)}, u32[]{:S(2)}) collective-permute-start(f32[12,48,128]{2,1,0:T(8,128)} %copy-done.23), channel_id=1, source_target_pairs={{0,224},{32,0},{64,32},{96,64},{128,96},{160,128},{192,160},{224,1... | collective-permute-start | bytes 884744 | tf_op jit(solution)/shard_map/cond/branch_0_fun/ppermute | solution.py:362
  29.1 13.0 %collective-permute-start.12 = (f32[12,48,128]{2,1,0:T(8,128)S(1)}, f32[12,48,128]{2,1,0:T(8,128)S(1)}, u32[]{:S(2)}, u32[]{:S(2)}) collective-permute-start(f32[12,48,128]{2,1,0:T(8,128)S(1)} %get-tuple-element.111), channel_id=1, source_target_pairs={{0,224},{32,0},{64,32},{96,64},{128,96},{160,128},{192,160},{224,1... | collective-permute-start | bytes 884744 | tf_op jit(solution)/shard_map/cond/branch_0_fun/ppermute | solution.py:362
  30.8 14.5 %collective-permute-start.2 = (f32[12,48,128]{2,1,0:T(8,128)}, f32[12,48,128]{2,1,0:T(8,128)S(1)}, u32[]{:S(2)}, u32[]{:S(2)}) collective-permute-start(f32[12,48,128]{2,1,0:T(8,128)} %copy-done.23), channel_id=1, source_target_pairs={{0,32},{32,64},{64,96},{96,128},{128,160},{160,192},{192,224},{224... | collective-permute-start | bytes 884744 | tf_op jit(solution)/shard_map/cond/branch_0_fun/ppermute | solution.py:362
  30.8 15.5 %collective-permute-start.3 = (f32[12,48,128]{2,1,0:T(8,128)}, f32[12,48,128]{2,1,0:T(8,128)S(1)}, u32[]{:S(2)}, u32[]{:S(2)}) collective-permute-start(f32[12,48,128]{2,1,0:T(8,128)} %copy-done.22), channel_id=1, source_target_pairs={{0,32},{32,64},{64,96},{96,128},{128,160},{160,192},{192,224},{224... | collective-permute-start | bytes 884744 | tf_op jit(solution)/shard_map/cond/branch_0_fun/ppermute | solution.py:362
  35.9 28.5 %copy-start.24 = (f32[12,48,128]{2,1,0:T(8,128)}, f32[12,48,128]{2,1,0:T(8,128)S(1)}, u32[]{:S(2)}) copy-start(f32[12,48,128]{2,1,0:T(8,128)S(1)} %collective-permute-done.8) | copy-start | bytes 884740 | tf_op jit(solution)/shard_map/cond
  35.9 12.6 %collective-permute-start.9 = (f32[12,48,128]{2,1,0:T(8,128)S(1)}, f32[12,48,128]{2,1,0:T(8,128)S(1)}, u32[]{:S(2)}, u32[]{:S(2)}) collective-permute-start(f32[12,48,128]{2,1,0:T(8,128)S(1)} %collective-permute-done.8), channel_id=1, source_target_pairs={{0,224},{32,0},{64,32},{96,64},{128,96},{160,128},{192,160},{224,1... | collective-permute-start | bytes 884744 | tf_op jit(solution)/shard_map/cond/branch_0_fun/ppermute | solution.py:362
  42.2 22.1 %copy-start.25 = (f32[12,48,128]{2,1,0:T(8,128)}, f32[12,48,128]{2,1,0:T(8,128)S(1)}, u32[]{:S(2)}) copy-start(f32[12,48,128]{2,1,0:T(8,128)S(1)} %collective-permute-done.12) | copy-start | bytes 884740 | tf_op jit(solution)/shard_map/cond
  42.2 12.7 %collective-permute-start.13 = (f32[12,48,128]{2,1,0:T(8,128)S(1)}, f32[12,48,128]{2,1,0:T(8,128)}, u32[]{:S(2)}, u32[]{:S(2)}) collective-permute-start(f32[12,48,128]{2,1,0:T(8,128)S(1)} %collective-permute-done.12), channel_id=1, source_target_pairs={{0,224},{32,0},{64,32},{96,64},{128,96},{160,128},{192,160},{224,1... | collective-permute-start | bytes 884744 | tf_op jit(solution)/shard_map/cond/branch_0_fun/ppermute | solution.py:362
  45.3 19.1 %copy-start.26 = (f32[12,48,128]{2,1,0:T(8,128)}, f32[12,48,128]{2,1,0:T(8,128)S(1)}, u32[]{:S(2)}) copy-start(f32[12,48,128]{2,1,0:T(8,128)S(1)} %collective-permute-done.2) | copy-start | bytes 884740 | tf_op jit(solution)/shard_map/cond
  45.3 12.7 %collective-permute-start.4 = (f32[12,48,128]{2,1,0:T(8,128)S(1)}, f32[12,48,128]{2,1,0:T(8,128)}, u32[]{:S(2)}, u32[]{:S(2)}) collective-permute-start(f32[12,48,128]{2,1,0:T(8,128)S(1)} %collective-permute-done.2), channel_id=1, source_target_pairs={{0,32},{32,64},{64,96},{96,128},{128,160},{160,192},{192,224},{224... | collective-permute-start | bytes 884744 | tf_op jit(solution)/shard_map/cond/branch_0_fun/ppermute | solution.py:362
  46.3 18.1 %copy-start.27 = (f32[12,48,128]{2,1,0:T(8,128)}, f32[12,48,128]{2,1,0:T(8,128)S(1)}, u32[]{:S(2)}) copy-start(f32[12,48,128]{2,1,0:T(8,128)S(1)} %collective-permute-done.3) | copy-start | bytes 884740 | tf_op jit(solution)/shard_map/cond
  46.3 13.2 %collective-permute-start.5 = (f32[12,48,128]{2,1,0:T(8,128)S(1)}, f32[12,48,128]{2,1,0:T(8,128)}, u32[]{:S(2)}, u32[]{:S(2)}) collective-permute-start(f32[12,48,128]{2,1,0:T(8,128)S(1)} %collective-permute-done.3), channel_id=1, source_target_pairs={{0,32},{32,64},{64,96},{96,128},{128,160},{160,192},{192,224},{224... | collective-permute-start | bytes 884744 | tf_op jit(solution)/shard_map/cond/branch_0_fun/ppermute | solution.py:362
  48.5 15.8 %copy-start.28 = (f32[12,48,128]{2,1,0:T(8,128)}, f32[12,48,128]{2,1,0:T(8,128)S(1)}, u32[]{:S(2)}) copy-start(f32[12,48,128]{2,1,0:T(8,128)S(1)} %collective-permute-done.9) | copy-start | bytes 884740 | tf_op jit(solution)/shard_map/cond
  48.5 12.7 %collective-permute-start.10 = (f32[12,48,128]{2,1,0:T(8,128)S(1)}, f32[12,48,128]{2,1,0:T(8,128)}, u32[]{:S(2)}, u32[]{:S(2)}) collective-permute-start(f32[12,48,128]{2,1,0:T(8,128)S(1)} %collective-permute-done.9), channel_id=1, source_target_pairs={{0,224},{32,0},{64,32},{96,64},{128,96},{160,128},{192,160},{224,1... | collective-permute-start | bytes 884744 | tf_op jit(solution)/shard_map/cond/branch_0_fun/ppermute | solution.py:362
  54.9 12.6 %collective-permute-start.14 = (f32[12,48,128]{2,1,0:T(8,128)}, f32[12,48,128]{2,1,0:T(8,128)}, u32[]{:S(2)}, u32[]{:S(2)}) collective-permute-start(f32[12,48,128]{2,1,0:T(8,128)} %collective-permute-done.13), channel_id=1, source_target_pairs={{0,224},{32,0},{64,32},{96,64},{128,96},{160,128},{192,160},{224,1... | collective-permute-start | bytes 884744 | tf_op jit(solution)/shard_map/cond/branch_0_fun/ppermute | solution.py:362
  58.0 9.6 %collective-permute-start.6 = (f32[12,48,128]{2,1,0:T(8,128)}, f32[12,48,128]{2,1,0:T(8,128)}, u32[]{:S(2)}, u32[]{:S(2)}) collective-permute-start(f32[12,48,128]{2,1,0:T(8,128)} %collective-permute-done.4), channel_id=1, source_target_pairs={{0,32},{32,64},{64,96},{96,128},{128,160},{160,192},{192,224},{224... | collective-permute-start | bytes 884744 | tf_op jit(solution)/shard_map/cond/branch_0_fun/ppermute | solution.py:362
  59.4 13.0 %collective-permute-start.7 = (f32[12,48,128]{2,1,0:T(8,128)}, f32[12,48,128]{2,1,0:T(8,128)}, u32[]{:S(2)}, u32[]{:S(2)}) collective-permute-start(f32[12,48,128]{2,1,0:T(8,128)} %collective-permute-done.5), channel_id=1, source_target_pairs={{0,32},{32,64},{64,96},{96,128},{128,160},{160,192},{192,224},{224... | collective-permute-start | bytes 884744 | tf_op jit(solution)/shard_map/cond/branch_0_fun/ppermute | solution.py:362
  61.3 12.6 %collective-permute-start.11 = (f32[12,48,128]{2,1,0:T(8,128)}, f32[12,48,128]{2,1,0:T(8,128)}, u32[]{:S(2)}, u32[]{:S(2)}) collective-permute-start(f32[12,48,128]{2,1,0:T(8,128)} %collective-permute-done.10), channel_id=1, source_target_pairs={{0,224},{32,0},{64,32},{96,64},{128,96},{160,128},{192,160},{224,1... | collective-permute-start | bytes 884744 | tf_op jit(solution)/shard_map/cond/branch_0_fun/ppermute | solution.py:362
  73.9 1.6 %copy-start.6 = (f32[32,192,128]{2,1,0:T(8,128)}, f32[32,192,128]{2,1,0:T(8,128)S(1)}, u32[]{:S(2)}) copy-start(f32[32,192,128]{2,1,0:T(8,128)S(1)} %all-to-all-done) | copy-start | bytes 9437188 | tf_op jit(solution)/shard_map/cond
  75.5 30.3 %copy-start.3 = (s32[2,1,256]{2,1,0:T(1,128)S(1)}, s32[2,1,256]{2,1,0:T(1,128)}, u32[]{:S(2)}) copy-start(s32[2,1,256]{2,1,0:T(1,128)} %broadcast_xor_fusion.labels_ref) | copy-start | bytes 6148 | tf_op jit(solution)/shard_map/cond
  107.4 15.0 %all-to-all-start.6 = ((f32[16,16,128]{2,1,0:T(8,128)}), f32[16,16,128]{2,1,0:T(8,128)S(1)}, u32[]{:S(2)}, u32[]{:S(2)}) async-start(f32[16,16,128]{2,1,0:T(8,128)} %bitcast.38), calls=%async_computation.6 | async-start | bytes 262144 | tf_op jit(solution)/shard_map/all_to_all | solution.py:320
